TPU v7x, 128 devices: a whole 4x4x4 slice. The times are simulated.
128 devices in a mesh: grp: 16 (over y, x), voc: 8 (over z, core).
Axes of the slice: x: 4, y: 4, z: 4, core: 2. Of those that a mesh axis runs over, the one named last changes fastest.
Arguments:
- teacher_rows: bfloat16 [512, 4096], P(('grp', 'voc')), may hold values from -125 to 125
- student_rows: bfloat16 [512, 4096], P(('grp', 'voc')), may hold values from -125 to 125
- teacher_head: bfloat16 [4096, 98304], P(None, ('grp', 'voc')), may hold values from -4 to 4
- student_head: bfloat16 [4096, 98304], P(None, ('grp', 'voc')), may hold values from -4 to 4
- response_ids: int32 [512], replicated, may hold values from 0 to 98303
- lengths: int32 [4], replicated, may hold values from 1 to 128, 384 in all
- seq_order: int32 [4], replicated, may hold values from 0 to 3, each once
Outputs:
- token_kl: float32 [512], P(('grp', 'voc'))
- sampled_gap: float32 [512], P(('grp', 'voc'))
- head_grad: bfloat16 [4096, 98304], P(None, ('grp', 'voc'))
- hidden_grad: bfloat16 [512, 4096], P(('grp', 'voc'))
Inputs may be any that keep to these rules, and one draw needn't show every extreme that they name: The lengths sum to exactly 384.
All inputs are finite; a program needn't handle non-finite values.
Results may differ from a plain program's by a relative error of at most 0.017.
Values may be sent and summed in bfloat16 or wider, within the bound.
No kernel may reach another device: no remote copies, remote signals or barrier semaphores. Data moves between devices by JAX's collectives and lax.ppermute only.
A program may use at most 128 MiB of HBM per device.

v0:
```python
import jax
import jax.numpy as jnp
from jax import lax
from jax.experimental import pallas as pl
from jax.experimental.pallas import tpu as pltpu
from jax.sharding import PartitionSpec as P

AXES = ("grp", "voc")
LOSS_SCALE = 64.0
SIDE = 4
CHIPS = SIDE**3
LARGE, SMALL = 58 * 1024 * 1024, 16 * 1024 * 1024
STUDENT, TEACHER = 47 * 1024 * 1024, 53 * 1024 * 1024
TILE = 256
TILES = 3
f32 = jnp.float32
bf16 = jnp.bfloat16


def at(y, x, z, c):
    return ((y * SIDE + x) * SIDE + z) * 2 + c


RANGE = range(SIDE)
PLANES = [[at(y, x, z, 0) for x in RANGE for z in RANGE] for y in RANGE] + [
    [at(y, x, z, 1) for y in RANGE for z in RANGE] for x in RANGE
]
CORES = [[2 * chip + c for chip in range(CHIPS)] for c in range(2)]
SWAP = [(i, i ^ 1) for i in range(2 * CHIPS)]
STEPS = (0, 1, 3, 2)


def along(step):
    pairs = []
    for y in RANGE:
        for x in RANGE:
            for z in RANGE:
                pairs.append((at(y, x, z, 0), at((y - step) % SIDE, x, z, 0)))
                pairs.append((at(y, x, z, 1), at(y, (x - step) % SIDE, z, 1)))
    return pairs


def swap(value):
    return lax.ppermute(value, AXES, SWAP)


def assemble(meta, pieces, rows, order):
    y, x, c = meta[0], meta[1], meta[2]
    half = pieces[0].shape[1]
    for index, piece in enumerate(pieces):
        step = STEPS[index % SIDE]
        kind = c if index < SIDE else 1 - c
        for p in range(SIDE):
            row = jnp.where(kind == 0, (y + step) % SIDE, p)
            col = jnp.where(kind == 0, p, (x + step) % SIDE)
            if order is not None:
                row = meta[order + row]
            first = pl.multiple_of((row * SIDE + col) * 32, 32)
            lane = pl.multiple_of(kind * half, half)
            rows[pl.ds(first, 32), pl.ds(lane, half)] = piece[32 * p : 32 * p + 32, :]


def pack(values, rows):
    lane = lax.broadcasted_iota(jnp.int32, (rows, 128), 1)
    packed = jnp.zeros((rows, 128), f32)
    for k, value in enumerate(values):
        packed = jnp.where(lane == k, value, packed)
    return packed


def row_sum(value):
    return jnp.sum(value, axis=1, keepdims=True)


def student_kernel(meta, *refs):
    pieces, (head, logits, scaled, stats, kept, rows, table, sem) = refs[:8], refs[8:]
    n = pl.program_id(0)
    total, width = logits.shape
    tile = head.shape[1]
    save = pltpu.make_async_copy(rows, kept, sem)

    @pl.when(n == 0)
    def _():
        assemble(meta, pieces, rows, None)
        save.start()

    logits[:, pl.ds(pl.multiple_of(n * tile, tile), tile)] = jnp.dot(
        rows[...], head[...], preferred_element_type=f32
    )

    @pl.when(n == pl.num_programs(0) - 1)
    def _():
        chunk = 64
        for i in range(total // chunk):
            here = slice(i * chunk, (i + 1) * chunk)
            s = logits[here, :]
            top = jnp.max(s, axis=1, keepdims=True)
            e = jnp.exp(s - top)
            scaled[here, :] = e
            table[here, :] = pack([top, row_sum(e)], chunk)
        stats[...] = table[...].T[:8]
        save.wait()


def teacher_kernel(meta, *refs):
    pieces, refs = refs[:8], refs[8:]
    head, student, scaled, ids, stats_s, spread, message, rows, teacher, moment, hit, tops = refs
    n = pl.program_id(0)
    total, tile = student.shape
    lanes = 128

    @pl.when(n == 0)
    def _():
        assemble(meta, pieces, rows, 4)
        moment[...] = jnp.zeros_like(moment)
        hit[...] = jnp.zeros_like(hit)
        tops[...] = jnp.full_like(tops, -jnp.inf)

    teacher[n] = jnp.dot(rows[...], head[...], preferred_element_type=f32)
    chunk = 64
    for i in range(total // chunk):
        here = slice(i * chunk, (i + 1) * chunk)
        own = ids[here, :] - meta[3] - n * tile
        for part in range(tile // lanes):
            side = slice(part * lanes, (part + 1) * lanes)
            t = teacher[n, here, side]
            gap = student[here, side] - t
            spread[here, side] = gap
            moment[here, :] += scaled[here, side] * gap
            column = part * lanes + lax.broadcasted_iota(jnp.int32, (chunk, lanes), 1)
            hit[here, :] += jnp.where(column == own, gap, 0.0)
            tops[here, :] = jnp.maximum(tops[here, :], t)

    @pl.when(n == pl.num_programs(0) - 1)
    def _():
        for i in range(total // chunk):
            here = slice(i * chunk, (i + 1) * chunk)
            top = jnp.max(tops[here, :], axis=1, keepdims=True)
            sums = jnp.exp(teacher[0, here, :] - top)
            for k in range(1, TILES):
                sums += jnp.exp(teacher[k, here, :] - top)
            moment[here, :] = pack(
                [row_sum(moment[here, :]), top, row_sum(sums), row_sum(hit[here, :])], chunk
            )
        moments = moment[...].T
        write_message(
            message,
            stats_s[0:1, :] + jnp.log(stats_s[1:2, :]),
            moments[0:1] / stats_s[1:2, :],
            moments[1:2] + jnp.log(moments[2:3]),
            moments[3:4],
        )


def logits_call(limit, kernel, meta, pieces, head, extra, extra_specs, out_shape, out_specs, scratch):
    total, (depth, width) = 4 * pieces[0].shape[0], head.shape
    once = pl.BlockSpec(pieces[0].shape, lambda n, m: (0, 0), pipeline_mode=pl.Buffered(1))
    return pl.pallas_call(
        kernel,
        grid_spec=pltpu.PrefetchScalarGridSpec(
            num_scalar_prefetch=1,
            grid=(TILES,),
            in_specs=[once] * 8 + [pl.BlockSpec((depth, TILE), lambda n, m: (0, n))] + extra_specs,
            out_specs=out_specs,
            scratch_shapes=scratch,
        ),
        out_shape=out_shape,
        compiler_params=params(limit),
        cost_estimate=cost(0, 0),
    )(meta, *pieces, head, *extra)


def turn_kernel(meta, own, far, turned):
    n = pl.program_id(0)
    count = pl.num_programs(0) // 2

    @pl.when(n < count)
    def _():
        turned[...] = own[...].T

    @pl.when(n >= count)
    def _():
        turned[...] = far[...].T


def turn_call(meta, head, far):
    half, width = far.shape
    block = 512
    count = half // block
    return pl.pallas_call(
        turn_kernel,
        grid_spec=pltpu.PrefetchScalarGridSpec(
            num_scalar_prefetch=1,
            grid=(2 * count,),
            in_specs=[
                pl.BlockSpec((block, width), lambda n, m: (m[2] * count + jnp.minimum(n, count - 1), 0)),
                pl.BlockSpec((block, width), lambda n, m: (jnp.maximum(n - count, 0), 0)),
            ],
            out_specs=pl.BlockSpec((width, block), lambda n, m: (n // count, n % count)),
        ),
        out_shape=jax.ShapeDtypeStruct((2 * width, half), bf16),
        compiler_params=params(LARGE),
        cost_estimate=cost(0, 8 * half * width),
    )(meta, head, far)


def stack_lines(values):
    line = lax.broadcasted_iota(jnp.int32, (128, values[0].shape[1]), 0)
    lines = jnp.zeros((128, values[0].shape[1]), f32)
    for k, value in enumerate(values):
        lines = jnp.where(line == k, value, lines)
    return lines


def write_message(message, lse, average, lse_t, hit):
    total = lse.shape[1]
    for k in range(4):
        here = slice(128 * k, 128 * (k + 1))
        for base, value in ((0, lse), (4, average)):
            lanes = slice(128 * (base + k), 128 * (base + k + 1))
            message[:, :, lanes] = jnp.broadcast_to(value[:, here].reshape(1, 1, 128), (CHIPS, 1, 128))
    line = lax.broadcasted_iota(jnp.int32, (128, total), 0) % 16
    values = jnp.where(line == 0, lse_t, jnp.where(line == 1, hit, 0.0)).T
    lane = lax.broadcasted_iota(jnp.int32, (total, 128), 1) // 16
    token = lax.broadcasted_iota(jnp.int32, (total, 128), 0) % 8
    values = jnp.where(lane == token, values, 0.0)
    message[:, :, 1024:1152] = jnp.sum(values.reshape(CHIPS, 8, 128), axis=1, keepdims=True)


def slab_places(meta):
    y, x, c = meta[0], meta[1], meta[2]
    places = []
    for slab in range(SIDE * SIDE):
        row, col = slab // SIDE, slab % SIDE
        step = jnp.where(c == 0, (row - y) % SIDE, (col - x) % SIDE)
        places.append(pl.multiple_of(32 * (SIDE * step + jnp.where(c == 0, col, row)), 32))
    return places


def grad_kernel(
    meta, scaled, spread, scaled_o, spread_o, stats, stats_o, gathered, gathered_o, grad, pair, merged
):
    total, width = grad.shape
    lse, average, live = [], [], []
    token = lax.broadcasted_iota(jnp.int32, (1, 128), 1)
    for k in range(4):
        both = (gathered, gathered_o)
        parts = [part[:, 0, 128 * k : 128 * (k + 1)] for part in both]
        top = jnp.max(jnp.maximum(*parts), axis=0, keepdims=True)
        factors = [jnp.exp(part - top) for part in parts]
        sums = jnp.sum(factors[0] + factors[1], axis=0, keepdims=True)
        lse.append(top + jnp.log(sums))
        moments = [part[:, 0, 512 + 128 * k : 640 + 128 * k] for part in both]
        moment = moments[0] * factors[0] + moments[1] * factors[1]
        average.append(jnp.sum(moment, axis=0, keepdims=True) / sums)
        live.append(jnp.where(token < meta[8 + k], LOSS_SCALE, 0.0))
    lse, average, live = (jnp.concatenate(value, axis=1) for value in (lse, average, live))
    own, far = (live * jnp.exp(top - lse) for top in (stats[0:1, :], stats_o[0:1, :]))
    lines = stack_lines([average, own, far, lse])
    merged[...] = lines[0:8]
    columns = lines.T
    for slab, first in enumerate(slab_places(meta)):
        rows = slice(32 * slab, 32 * slab + 32)
        for side, (e, gap) in enumerate(((scaled, spread), (scaled_o, spread_o))):
            value = (
                columns[rows, side + 1 : side + 2] * e[rows, :] * (gap[rows, :] - columns[rows, 0:1])
            ).astype(bf16)
            if side == 0:
                grad[rows, :] = value
            pair[pl.ds(first, 32), side * width : (side + 1) * width] = value


def params(limit):
    return pltpu.CompilerParams(vmem_limit_bytes=limit)


def cost(flops, moved):
    return pl.CostEstimate(flops=flops, bytes_accessed=moved, transcendentals=0)


def body(teacher_rows, student_rows, teacher_head, student_head, response_ids, lengths, seq_order):
    depth, width = student_head.shape
    half = depth // 2
    total = response_ids.shape[0]
    own = student_rows.shape[0]
    place = lax.axis_index(AXES)
    c, x, y = place % 2, (place // 8) % SIDE, place // 32

    both = jnp.concatenate([student_rows, teacher_rows], axis=0)
    mine = lax.dynamic_slice_in_dim(both, c * half, half, axis=1)
    theirs = swap(lax.dynamic_slice_in_dim(both, (1 - c) * half, half, axis=1))

    def shard(a, b):
        return jnp.where(c == 0, jnp.concatenate([a, b]), jnp.concatenate([b, a]))

    shards = jnp.stack([shard(mine[:own], theirs[:own]), shard(mine[own:], theirs[own:])])
    wide = jnp.broadcast_to(shards[None], (SIDE * SIDE,) + shards.shape)
    wide = lax.all_to_all(wide, AXES, 0, 0, axis_index_groups=PLANES, tiled=True)

    position = jnp.arange(4, dtype=jnp.int32)
    inverse = jnp.sum(jnp.where(seq_order[None, :] == position[:, None], position[None, :], 0), axis=1)
    meta = jnp.concatenate([jnp.stack([y, x, c, place * width]).astype(jnp.int32), inverse, lengths])
    ids = response_ids[:, None]
    far = lax.dynamic_slice_in_dim(student_head, (1 - c) * half, half)
    wide, meta, ids, far = lax.optimization_barrier((wide, meta, ids, far))
    far = swap(far)

    def along_axis(plane, relay=False):
        after, before = (lax.ppermute(plane, AXES, along(step)) for step in (1, 3))
        if relay:
            return [plane, after, before, lax.ppermute(after, AXES, along(1))]
        return [plane, after, before, lax.ppermute(plane, AXES, along(2))]

    student_pieces = along_axis(wide[:, 0].reshape(-1, half))
    teacher_pieces = along_axis(wide[:, 1].reshape(-1, half), True)
    turned = turn_call(meta, student_head, far)
    near = swap(teacher_pieces[0])
    student_pieces, turned, near = lax.optimization_barrier((student_pieces, turned, near))
    student_pieces += [swap(piece) for piece in student_pieces]

    fixed = lambda shape: pl.BlockSpec(shape, lambda n, m: (0,) * len(shape))
    moving = pl.BlockSpec((total, TILE), lambda n, m: (0, n))
    square = jax.ShapeDtypeStruct((total, width), f32)
    line = jax.ShapeDtypeStruct((8, total), f32)
    logits, scaled, stats_s, rows = logits_call(
        STUDENT, student_kernel, meta, student_pieces, student_head, [], [],
        [square, square, line, jax.ShapeDtypeStruct((total, depth), bf16)],
        [fixed((total, width)), fixed((total, width)), fixed((8, total)), pl.BlockSpec(memory_space=pl.ANY)],
        [pltpu.VMEM((total, depth), bf16), pltpu.VMEM((total, 128), f32), pltpu.SemaphoreType.DMA],
    )
    teacher_pieces, stats_s = lax.optimization_barrier((teacher_pieces, stats_s))
    teacher_pieces += [near] + [swap(piece) for piece in teacher_pieces[1:]]
    spread, message = logits_call(
        TEACHER, teacher_kernel, meta, teacher_pieces, teacher_head,
        [logits, scaled, ids, stats_s], [moving, moving, fixed((total, 1)), fixed((8, total))],
        [square, jax.ShapeDtypeStruct((CHIPS, 1, 1152), f32)],
        [moving, fixed((CHIPS, 1, 1152))],
        [pltpu.VMEM((total, depth), bf16), pltpu.VMEM((TILES, total, TILE), f32)]
        + [pltpu.VMEM((total, 128), f32)] * 3,
    )

    gathered = lax.all_to_all(message, AXES, 0, 0, axis_index_groups=CORES, tiled=True)
    scaled, spread, stats_s = lax.optimization_barrier((scaled, spread, stats_s))
    scaled_o, spread_o, stats_o = swap(scaled), swap(spread), swap(stats_s)
    gathered_o = swap(gathered)
    in_vmem = pl.BlockSpec(memory_space=pltpu.VMEM)
    grad, pair, merged = pl.pallas_call(
        grad_kernel,
        in_specs=[pl.BlockSpec(memory_space=pltpu.SMEM)] + [in_vmem] * 8,
        out_specs=[in_vmem] * 3,
        out_shape=[
            jax.ShapeDtypeStruct((total, width), bf16),
            jax.ShapeDtypeStruct((total, 2 * width), bf16),
            jax.ShapeDtypeStruct((8, total), f32),
        ],
        compiler_params=params(SMALL),
        cost_estimate=cost(10 * total * width, 20 * total * width),
    )(meta, scaled, spread, scaled_o, spread_o, stats_s, stats_o, gathered, gathered_o)
    gathered, gathered_o, merged = lax.optimization_barrier((gathered, gathered_o, merged))
    blocks = jnp.dot(pair, turned, preferred_element_type=f32).astype(bf16)
    blocks = blocks.reshape(SIDE, total // SIDE, half)
    kept = blocks[0].astype(f32)
    for step in STEPS[:0:-1]:
        kept = kept + lax.ppermute(blocks[step], AXES, along(SIDE - step)).astype(f32)
    parts = lax.all_to_all(kept.astype(bf16), AXES, 0, 0, axis_index_groups=PLANES, tiled=True)
    head_grad = lax.dot_general(
        rows, grad, (((0,), (0,)), ((), ())), preferred_element_type=f32
    ).astype(bf16)
    mine = jnp.sum(parts.reshape(SIDE * SIDE, 8, half).astype(f32), axis=0).astype(bf16)
    mine, head_grad = lax.optimization_barrier((mine, head_grad))
    keep = lax.dynamic_slice_in_dim(mine, c * own, own)
    take = swap(lax.dynamic_slice_in_dim(mine, (1 - c) * own, own))
    hidden_grad = jnp.where(
        c == 0, jnp.concatenate([keep, take], axis=1), jnp.concatenate([take, keep], axis=1)
    )

    start = place * own
    mine = lax.dynamic_slice_in_dim(merged, start, own, axis=1)
    average, student_lse = mine[0], mine[3]
    teach = jnp.concatenate([gathered[:, 0, 1024:], gathered_o[:, 0, 1024:]]).reshape(2 * CHIPS, 8, 16)
    teach = lax.dynamic_slice_in_dim(teach, c * own, own, axis=1)
    teacher_lse = jax.nn.logsumexp(teach[:, :, 0], axis=0)
    hit = jnp.sum(teach[:, :, 1], axis=0)
    span = total // lengths.shape[0]
    index = start + jnp.arange(own, dtype=jnp.int32)
    live = (index % span < lengths[index // span]).astype(f32)
    token_kl = live * (average - student_lse + teacher_lse)
    sampled_gap = live * (hit - student_lse + teacher_lse)
    return (token_kl, sampled_gap, head_grad, hidden_grad)


def solution(mesh):
    in_specs = (P(AXES, None), P(AXES, None), P(None, AXES), P(None, AXES), P(), P(), P())
    out_specs = (P(AXES), P(AXES), P(None, AXES), P(AXES, None))
    return jax.shard_map(body, mesh=mesh, in_specs=in_specs, out_specs=out_specs, check_vma=False)
```

profile of v0, /device:TPU:1, one launch (start us, length us, event | category | flops | bytes accessed | tf_op | source)
XLA Modules:
  0.0 143.6 jit_solution(15418379723303323180)
XLA Ops:
  1.6 1.5 %collective-permute-start = (bf16[8,2048]{1,0:T(8,128)(2,1)S(1)}, bf16[8,2048]{1,0:T(8,128)(2,1)S(1)}, u32[]{:S(2)}, u32[]{:S(2)}) collective-permute-start(bf16[8,2048]{1,0:T(8,128)(2,1)S(1)} %get-tuple-element.78), channel_id=1, source_target_pairs={{0,1},{1,0},{2,3},{3,2},{4,5},{5,4},{6,7},{7,6},{8,9},{9,8},{10,11... | collective-permute-start | bytes 98312 | tf_op jit(solution)/shard_map/ppermute | solution.py:44
  5.1 7.9 %all-to-all-start = ((bf16[16,2,8,2048]{3,2,1,0:T(8,128)(2,1)}), bf16[16,2,8,2048]{3,2,1,0:T(8,128)(2,1)S(1)}, u32[]{:S(2)}, u32[]{:S(2)}) async-start(bf16[16,2,8,2048]{3,2,1,0:T(8,128)(2,1)} %broadcast_in_dim.16), calls=%async_computation | async-start | bytes 2097152 | tf_op jit(solution)/shard_map/all_to_all | solution.py:298
  13.8 3.8 %constant_dynamic-slice_fusion.3 = bf16[2048,768]{1,0:T(8,128)(2,1)} fusion(bf16[4096,768]{1,0:T(8,128)(2,1)} %refs_8_.2, s32[]{:T(128)S(6)} %select_n.114), kind=kLoop, calls=%fused_computation.30 | loop fusion | bytes 6291460 | tf_op jit(solution)/shard_map/dynamic_slice | solution.py:304
  17.5 10.1 %all-to-all-done = bf16[16,2,8,2048]{3,2,1,0:T(8,128)(2,1)S(1)} async-done(((bf16[16,2,8,2048]{3,2,1,0:T(8,128)(2,1)}), bf16[16,2,8,2048]{3,2,1,0:T(8,128)(2,1)S(1)}, u32[]{:S(2)}, u32[]{:S(2)}) %all-to-all-start) | async-done | bytes 1048608 | tf_op jit(solution)/shard_map/all_to_all | solution.py:298
  29.1 2.2 %collective-permute-start.4 = (bf16[128,2048]{1,0:T(8,128)(2,1)S(1)}, bf16[128,2048]{1,0:T(8,128)(2,1)S(1)}, u32[]{:S(2)}, u32[]{:S(2)}) collective-permute-start(bf16[128,2048]{1,0:T(8,128)(2,1)S(1)} %get-tuple-element.39.refs_0_), channel_id=1, source_target_pairs={{0,96},{1,25},{2,98},{3,27},{4,100},{5,29},{6,102},{7,31},{8,104},... | collective-permute-start | bytes 1572872 | tf_op jit(solution)/shard_map/ppermute | solution.py:309
  31.3 1.7 %collective-permute-start.6 = (bf16[128,2048]{1,0:T(8,128)(2,1)S(1)}, bf16[128,2048]{1,0:T(8,128)(2,1)S(1)}, u32[]{:S(2)}, u32[]{:S(2)}) collective-permute-start(bf16[128,2048]{1,0:T(8,128)(2,1)S(1)} %get-tuple-element.39.refs_0_), channel_id=1, source_target_pairs={{0,64},{1,17},{2,66},{3,19},{4,68},{5,21},{6,70},{7,23},{8,72},{9,... | collective-permute-start | bytes 1572872 | tf_op jit(solution)/shard_map/ppermute | solution.py:312
  34.6 2.1 %collective-permute-start.1 = (bf16[128,2048]{1,0:T(8,128)(2,1)S(1)}, bf16[128,2048]{1,0:T(8,128)(2,1)S(1)}, u32[]{:S(2)}, u32[]{:S(2)}) collective-permute-start(bf16[128,2048]{1,0:T(8,128)(2,1)S(1)} %get-tuple-element.44.refs_0_), channel_id=1, source_target_pairs={{0,96},{1,25},{2,98},{3,27},{4,100},{5,29},{6,102},{7,31},{8,104},... | collective-permute-start | bytes 1572872 | tf_op jit(solution)/shard_map/ppermute | solution.py:309
  36.8 9.2 %shard_map.102 = bf16[1536,2048]{1,0:T(8,128)(2,1)} custom-call(s32[12]{0:T(128)} %concatenate.77.meta, bf16[4096,768]{1,0:T(8,128)(2,1)} %refs_8_.2, bf16[2048,768]{1,0:T(8,128)(2,1)} %collective-permute-done.7.far), custom_call_target="tpu_custom_call" | custom-call | bytes 12582912 | tf_op jit(solution)/shard_map/pallas_call | solution.py:190
  49.6 2.3 %collective-permute-start.3 = (bf16[128,2048]{1,0:T(8,128)(2,1)S(1)}, bf16[128,2048]{1,0:T(8,128)(2,1)S(1)}, u32[]{:S(2)}, u32[]{:S(2)}) collective-permute-start(bf16[128,2048]{1,0:T(8,128)(2,1)S(1)} %collective-permute-done.1.refs_1_), channel_id=1, source_target_pairs={{0,96},{1,25},{2,98},{3,27},{4,100},{5,29},{6,102},{7,31},{8,104},... | collective-permute-start | bytes 1572872 | tf_op jit(solution)/shard_map/ppermute | solution.py:311
  51.9 8.5 %shard_map.103 = (f32[512,768]{1,0:T(8,128)S(1)}, f32[512,768]{1,0:T(8,128)}, f32[8,512]{1,0:T(8,128)S(1)}, bf16[512,4096]{1,0:T(8,128)(2,1)}) custom-call(s32[12]{0:T(128)S(1)} %copy-done.3, bf16[128,2048]{1,0:T(8,128)(2,1)S(1)} %get-tuple-element.39.refs_0_, bf16[128,2048]{1,0:T(8,128)(2,1)S(1)} %collective-permute-done.4.refs_1_, ...), custom_call_target="tpu_custom_call" | custom-call | tf_op jit(solution)/shard_map/pallas_call | solution.py:158
  61.6 1.4 collective-permute-start.13
  66.9 10.7 %shard_map.104 = (f32[512,768]{1,0:T(8,128)}, f32[64,1,1152]{2,1,0:T(1,128)S(1)}) custom-call(s32[12]{0:T(128)S(1)} %copy-done.3, bf16[128,2048]{1,0:T(8,128)(2,1)} %copy-done.8, bf16[128,2048]{1,0:T(8,128)(2,1)} %copy-done.10, bf16[128,2048]{1,0:T(8,128)(2,1)} %copy-done.11, bf16[128,2048]{1,0:T(8,128)(2,1)} %copy-done.12, bf16[128,2048]{1,0:T(8,128)(2,1)} %copy-done.9, ...), custom_call_target="tpu_custom_call" | custom-call | tf_op jit(solution)/shard_map/pallas_call | solution.py:158
  78.2 17.6 %all_to_all.19.gathered = f32[64,1,1152]{2,1,0:T(1,128)S(1)} all-to-all(f32[64,1,1152]{2,1,0:T(1,128)S(1)} %get-tuple-element.53), channel_id=1, replica_groups={{0,2,4,6,8,10,12,14,16,18,20,22,24,26,28,30,32,34,36,38,40,42,44,46,48,..., dimensions={0} | all-to-all | bytes 589824 | tf_op jit(solution)/shard_map/all_to_all | solution.py:342
  95.8 1.6 %collective-permute-start.16 = (f32[64,1,1152]{2,1,0:T(1,128)S(1)}, f32[64,1,1152]{2,1,0:T(1,128)}, u32[]{:S(2)}, u32[]{:S(2)}) collective-permute-start(f32[64,1,1152]{2,1,0:T(1,128)S(1)} %all_to_all.19.gathered), channel_id=1, source_target_pairs={{0,1},{1,0},{2,3},{3,2},{4,5},{5,4},{6,7},{7,6},{8,9},{9,8},{10,11... | collective-permute-start | bytes 884744 | tf_op jit(solution)/shard_map/ppermute | solution.py:44
  100.2 2.7 %shard_map.105 = (bf16[512,768]{1,0:T(8,128)(2,1)S(1)}, bf16[512,1536]{1,0:T(8,128)(2,1)S(1)}, f32[8,512]{1,0:T(8,128)S(1)}) custom-call(s32[12]{0:T(128)S(1)} %copy-done.3, f32[512,768]{1,0:T(8,128)S(1)} %copy-done, f32[512,768]{1,0:T(8,128)S(1)} %copy-done.1, f32[512,768]{1,0:T(8,128)S(1)} %collective-permute-done.17.scaled_o, ...), custom_call_target="tpu_custom_call" | custom-call | flops 3932160 | bytes 7864320 | tf_op jit(solution)/shard_map/pallas_call | solution.py:347
  103.9 3.6 %convolution_convert_fusion.1 = bf16[512,2048]{1,0:T(8,128)(2,1)S(1)} fusion(bf16[512,1536]{1,0:T(8,128)(2,1)S(1)} %get-tuple-element.62, bf16[1536,2048]{1,0:T(8,128)(2,1)S(1)} %copy-done.7), kind=kOutput, calls=%fused_computation.2 | convolution fusion | flops 3222274048 | bytes 9961472 | tf_op jit(solution)/shard_map/dot_general | solution.py:360
  109.2 2.1 %collective-permute-start.21 = (bf16[128,2048]{1,0:T(8,128)(2,1)}, bf16[128,2048]{1,0:T(8,128)(2,1)}, u32[]{:S(2)}, u32[]{:S(2)}) collective-permute-start(bf16[128,2048]{1,0:T(8,128)(2,1)} %get-tuple-element.74), channel_id=1, source_target_pairs={{0,96},{1,25},{2,98},{3,27},{4,100},{5,29},{6,102},{7,31},{8,104},... | collective-permute-start | bytes 1572872 | tf_op jit(solution)/shard_map/ppermute | solution.py:364
  113.4 5.5 %collective-permute-done.20 = bf16[128,2048]{1,0:T(8,128)(2,1)} collective-permute-done((bf16[128,2048]{1,0:T(8,128)(2,1)}, bf16[128,2048]{1,0:T(8,128)(2,1)}, u32[]{:S(2)}, u32[]{:S(2)}) %collective-permute-start.20) | collective-permute-done | bytes 524320 | tf_op jit(solution)/shard_map/ppermute | solution.py:364
  118.8 3.6 %collective-permute-done.21 = bf16[128,2048]{1,0:T(8,128)(2,1)} collective-permute-done((bf16[128,2048]{1,0:T(8,128)(2,1)}, bf16[128,2048]{1,0:T(8,128)(2,1)}, u32[]{:S(2)}, u32[]{:S(2)}) %collective-permute-start.21) | collective-permute-done | bytes 524320 | tf_op jit(solution)/shard_map/ppermute | solution.py:364
  122.5 2.0 %collective-permute-done.22 = bf16[128,2048]{1,0:T(8,128)(2,1)} collective-permute-done((bf16[128,2048]{1,0:T(8,128)(2,1)}, bf16[128,2048]{1,0:T(8,128)(2,1)}, u32[]{:S(2)}, u32[]{:S(2)}) %collective-permute-start.22) | collective-permute-done | bytes 524320 | tf_op jit(solution)/shard_map/ppermute | solution.py:364
  124.4 2.5 %fusion = bf16[16,8,2048]{2,1,0:T(8,128)(2,1)} fusion(bf16[128,2048]{1,0:T(8,128)(2,1)} %collective-permute-done.22, bf16[128,2048]{1,0:T(8,128)(2,1)} %collective-permute-done.21, bf16[128,2048]{1,0:T(8,128)(2,1)} %collective-permute-done.20, bf16[512,2048]{1,0:T(8,128)(2,1)S(1)} %convolution_convert_fusion.1), kind=kLoop, calls=%fused_computation.4 | loop fusion | flops 2097152 | bytes 2621440 | tf_op jit(solution)/shard_map/all_to_all | solution.py:365
  126.9 3.6 %all-to-all-start.2 = ((bf16[16,8,2048]{2,1,0:T(8,128)(2,1)}), bf16[16,8,2048]{2,1,0:T(8,128)(2,1)S(1)}, u32[]{:S(2)}, u32[]{:S(2)}) async-start(bf16[16,8,2048]{2,1,0:T(8,128)(2,1)} %fusion), calls=%async_computation.2 | async-start | bytes 1048576 | tf_op jit(solution)/shard_map/all_to_all | solution.py:365
  130.5 8.4 %convolution_convert_fusion = bf16[4096,768]{1,0:T(8,128)(2,1)} fusion(bf16[512,4096]{1,0:T(8,128)(2,1)} %get-tuple-element.64, bf16[512,768]{1,0:T(8,128)(2,1)S(1)} %copy-done.5), kind=kOutput, calls=%fused_computation.1 | convolution fusion | flops 3224371200 | bytes 11272192 | tf_op jit(solution)/shard_map/dot_general | solution.py:366
  140.2 1.9 %collective-permute-start.23 = (bf16[4,2048]{1,0:T(4,128)(2,1)S(1)}, bf16[4,2048]{1,0:T(4,128)(2,1)S(1)}, u32[]{:S(2)}, u32[]{:S(2)}) collective-permute-start(bf16[4,2048]{1,0:T(4,128)(2,1)S(1)} %get-tuple-element.80), channel_id=1, source_target_pairs={{0,1},{1,0},{2,3},{3,2},{4,5},{5,4},{6,7},{7,6},{8,9},{9,8},{10,11... | collective-permute-start | bytes 49160 | tf_op jit(solution)/shard_map/ppermute | solution.py:44
  (101 shorter events, 26.2 us)
Async XLA Ops:
  1.6 2.4 %collective-permute-start = (bf16[8,2048]{1,0:T(8,128)(2,1)S(1)}, bf16[8,2048]{1,0:T(8,128)(2,1)S(1)}, u32[]{:S(2)}, u32[]{:S(2)}) collective-permute-start(bf16[8,2048]{1,0:T(8,128)(2,1)S(1)} %get-tuple-element.78), channel_id=1, source_target_pairs={{0,1},{1,0},{2,3},{3,2},{4,5},{5,4},{6,7},{7,6},{8,9},{9,8},{10,11... | collective-permute-start | bytes 98312 | tf_op jit(solution)/shard_map/ppermute | solution.py:44
  5.1 22.5 %all-to-all-start = ((bf16[16,2,8,2048]{3,2,1,0:T(8,128)(2,1)}), bf16[16,2,8,2048]{3,2,1,0:T(8,128)(2,1)S(1)}, u32[]{:S(2)}, u32[]{:S(2)}) async-start(bf16[16,2,8,2048]{3,2,1,0:T(8,128)(2,1)} %broadcast_in_dim.16), calls=%async_computation | async-start | bytes 2097152 | tf_op jit(solution)/shard_map/all_to_all | solution.py:298
  27.6 7.0 %collective-permute-start.7 = (bf16[2048,768]{1,0:T(8,128)(2,1)}, bf16[2048,768]{1,0:T(8,128)(2,1)}, u32[]{:S(2)}, u32[]{:S(2)}) collective-permute-start(bf16[2048,768]{1,0:T(8,128)(2,1)} %constant_dynamic-slice_fusion.3), channel_id=1, source_target_pairs={{0,1},{1,0},{2,3},{3,2},{4,5},{5,4},{6,7},{7,6},{8,9},{9,8},{10,11... | collective-permute-start | bytes 9437192 | tf_op jit(solution)/shard_map/ppermute | solution.py:44
  29.1 16.9 %collective-permute-start.4 = (bf16[128,2048]{1,0:T(8,128)(2,1)S(1)}, bf16[128,2048]{1,0:T(8,128)(2,1)S(1)}, u32[]{:S(2)}, u32[]{:S(2)}) collective-permute-start(bf16[128,2048]{1,0:T(8,128)(2,1)S(1)} %get-tuple-element.39.refs_0_), channel_id=1, source_target_pairs={{0,96},{1,25},{2,98},{3,27},{4,100},{5,29},{6,102},{7,31},{8,104},... | collective-permute-start | bytes 1572872 | tf_op jit(solution)/shard_map/ppermute | solution.py:309
  31.3 15.2 %collective-permute-start.5 = (bf16[128,2048]{1,0:T(8,128)(2,1)S(1)}, bf16[128,2048]{1,0:T(8,128)(2,1)S(1)}, u32[]{:S(2)}, u32[]{:S(2)}) collective-permute-start(bf16[128,2048]{1,0:T(8,128)(2,1)S(1)} %get-tuple-element.39.refs_0_), channel_id=1, source_target_pairs={{0,32},{1,9},{2,34},{3,11},{4,36},{5,13},{6,38},{7,15},{8,40},{9,1... | collective-permute-start | bytes 1572872 | tf_op jit(solution)/shard_map/ppermute | solution.py:309
  31.3 15.2 %collective-permute-start.6 = (bf16[128,2048]{1,0:T(8,128)(2,1)S(1)}, bf16[128,2048]{1,0:T(8,128)(2,1)S(1)}, u32[]{:S(2)}, u32[]{:S(2)}) collective-permute-start(bf16[128,2048]{1,0:T(8,128)(2,1)S(1)} %get-tuple-element.39.refs_0_), channel_id=1, source_target_pairs={{0,64},{1,17},{2,66},{3,19},{4,68},{5,21},{6,70},{7,23},{8,72},{9,... | collective-permute-start | bytes 1572872 | tf_op jit(solution)/shard_map/ppermute | solution.py:312
  33.0 13.4 %collective-permute-start.8 = (bf16[128,2048]{1,0:T(8,128)(2,1)S(1)}, bf16[128,2048]{1,0:T(8,128)(2,1)S(1)}, u32[]{:S(2)}, u32[]{:S(2)}) collective-permute-start(bf16[128,2048]{1,0:T(8,128)(2,1)S(1)} %get-tuple-element.44.refs_0_), channel_id=1, source_target_pairs={{0,1},{1,0},{2,3},{3,2},{4,5},{5,4},{6,7},{7,6},{8,9},{9,8},{10,11... | collective-permute-start | bytes 1572872 | tf_op jit(solution)/shard_map/ppermute | solution.py:44
  34.6 14.1 %collective-permute-start.1 = (bf16[128,2048]{1,0:T(8,128)(2,1)S(1)}, bf16[128,2048]{1,0:T(8,128)(2,1)S(1)}, u32[]{:S(2)}, u32[]{:S(2)}) collective-permute-start(bf16[128,2048]{1,0:T(8,128)(2,1)S(1)} %get-tuple-element.44.refs_0_), channel_id=1, source_target_pairs={{0,96},{1,25},{2,98},{3,27},{4,100},{5,29},{6,102},{7,31},{8,104},... | collective-permute-start | bytes 1572872 | tf_op jit(solution)/shard_map/ppermute | solution.py:309
  46.5 3.1 %collective-permute-start.10 = (bf16[128,2048]{1,0:T(8,128)(2,1)S(1)}, bf16[128,2048]{1,0:T(8,128)(2,1)S(1)}, u32[]{:S(2)}, u32[]{:S(2)}) collective-permute-start(bf16[128,2048]{1,0:T(8,128)(2,1)S(1)} %collective-permute-done.4.refs_1_), channel_id=1, source_target_pairs={{0,1},{1,0},{2,3},{3,2},{4,5},{5,4},{6,7},{7,6},{8,9},{9,8},{10,11... | collective-permute-start | bytes 1572872 | tf_op jit(solution)/shard_map/ppermute | solution.py:44
  47.6 4.3 %collective-permute-start.11 = (bf16[128,2048]{1,0:T(8,128)(2,1)S(1)}, bf16[128,2048]{1,0:T(8,128)(2,1)S(1)}, u32[]{:S(2)}, u32[]{:S(2)}) collective-permute-start(bf16[128,2048]{1,0:T(8,128)(2,1)S(1)} %collective-permute-done.5.refs_2_), channel_id=1, source_target_pairs={{0,1},{1,0},{2,3},{3,2},{4,5},{5,4},{6,7},{7,6},{8,9},{9,8},{10,11... | collective-permute-start | bytes 1572872 | tf_op jit(solution)/shard_map/ppermute | solution.py:44
  47.7 4.2 %collective-permute-start.12 = (bf16[128,2048]{1,0:T(8,128)(2,1)S(1)}, bf16[128,2048]{1,0:T(8,128)(2,1)S(1)}, u32[]{:S(2)}, u32[]{:S(2)}) collective-permute-start(bf16[128,2048]{1,0:T(8,128)(2,1)S(1)} %collective-permute-done.6.refs_3_), channel_id=1, source_target_pairs={{0,1},{1,0},{2,3},{3,2},{4,5},{5,4},{6,7},{7,6},{8,9},{9,8},{10,11... | collective-permute-start | bytes 1572872 | tf_op jit(solution)/shard_map/ppermute | solution.py:44
  48.1 3.8 %collective-permute-start.9 = (bf16[128,2048]{1,0:T(8,128)(2,1)S(1)}, bf16[128,2048]{1,0:T(8,128)(2,1)S(1)}, u32[]{:S(2)}, u32[]{:S(2)}) collective-permute-start(bf16[128,2048]{1,0:T(8,128)(2,1)S(1)} %get-tuple-element.39.refs_0_), channel_id=1, source_target_pairs={{0,1},{1,0},{2,3},{3,2},{4,5},{5,4},{6,7},{7,6},{8,9},{9,8},{10,11... | collective-permute-start | bytes 1572872 | tf_op jit(solution)/shard_map/ppermute | solution.py:44
  48.8 12.8 %collective-permute-start.2 = (bf16[128,2048]{1,0:T(8,128)(2,1)S(1)}, bf16[128,2048]{1,0:T(8,128)(2,1)S(1)}, u32[]{:S(2)}, u32[]{:S(2)}) collective-permute-start(bf16[128,2048]{1,0:T(8,128)(2,1)S(1)} %get-tuple-element.44.refs_0_), channel_id=1, source_target_pairs={{0,32},{1,9},{2,34},{3,11},{4,36},{5,13},{6,38},{7,15},{8,40},{9,1... | collective-permute-start | bytes 1572872 | tf_op jit(solution)/shard_map/ppermute | solution.py:309
  49.6 12.0 %collective-permute-start.3 = (bf16[128,2048]{1,0:T(8,128)(2,1)S(1)}, bf16[128,2048]{1,0:T(8,128)(2,1)S(1)}, u32[]{:S(2)}, u32[]{:S(2)}) collective-permute-start(bf16[128,2048]{1,0:T(8,128)(2,1)S(1)} %collective-permute-done.1.refs_1_), channel_id=1, source_target_pairs={{0,96},{1,25},{2,98},{3,27},{4,100},{5,29},{6,102},{7,31},{8,104},... | collective-permute-start | bytes 1572872 | tf_op jit(solution)/shard_map/ppermute | solution.py:311
  61.6 3.0 %collective-permute-start.13 = (bf16[128,2048]{1,0:T(8,128)(2,1)S(1)}, bf16[128,2048]{1,0:T(8,128)(2,1)S(1)}, u32[]{:S(2)}, u32[]{:S(2)}) collective-permute-start(bf16[128,2048]{1,0:T(8,128)(2,1)S(1)} %collective-permute-done.1.refs_1_), channel_id=1, source_target_pairs={{0,1},{1,0},{2,3},{3,2},{4,5},{5,4},{6,7},{7,6},{8,9},{9,8},{10,11... | collective-permute-start | bytes 1572872 | tf_op jit(solution)/shard_map/ppermute | solution.py:44
  63.2 2.9 %collective-permute-start.15 = (bf16[128,2048]{1,0:T(8,128)(2,1)S(1)}, bf16[128,2048]{1,0:T(8,128)(2,1)S(1)}, u32[]{:S(2)}, u32[]{:S(2)}) collective-permute-start(bf16[128,2048]{1,0:T(8,128)(2,1)S(1)} %collective-permute-done.3.refs_3_), channel_id=1, source_target_pairs={{0,1},{1,0},{2,3},{3,2},{4,5},{5,4},{6,7},{7,6},{8,9},{9,8},{10,11... | collective-permute-start | bytes 1572872 | tf_op jit(solution)/shard_map/ppermute | solution.py:44
  77.6 21.1 %collective-permute-start.17 = (f32[512,768]{1,0:T(8,128)S(1)}, f32[512,768]{1,0:T(8,128)S(1)}, u32[]{:S(2)}, u32[]{:S(2)}) collective-permute-start(f32[512,768]{1,0:T(8,128)S(1)} %copy-done), channel_id=1, source_target_pairs={{0,1},{1,0},{2,3},{3,2},{4,5},{5,4},{6,7},{7,6},{8,9},{9,8},{10,11... | collective-permute-start | bytes 4718600 | tf_op jit(solution)/shard_map/ppermute | solution.py:44
  78.1 20.7 %collective-permute-start.18 = (f32[512,768]{1,0:T(8,128)}, f32[512,768]{1,0:T(8,128)}, u32[]{:S(2)}, u32[]{:S(2)}) collective-permute-start(f32[512,768]{1,0:T(8,128)} %get-tuple-element.56.spread), channel_id=1, source_target_pairs={{0,1},{1,0},{2,3},{3,2},{4,5},{5,4},{6,7},{7,6},{8,9},{9,8},{10,11... | collective-permute-start | bytes 4718600 | tf_op jit(solution)/shard_map/ppermute | solution.py:44
  95.8 3.0 %collective-permute-start.16 = (f32[64,1,1152]{2,1,0:T(1,128)S(1)}, f32[64,1,1152]{2,1,0:T(1,128)}, u32[]{:S(2)}, u32[]{:S(2)}) collective-permute-start(f32[64,1,1152]{2,1,0:T(1,128)S(1)} %all_to_all.19.gathered), channel_id=1, source_target_pairs={{0,1},{1,0},{2,3},{3,2},{4,5},{5,4},{6,7},{7,6},{8,9},{9,8},{10,11... | collective-permute-start | bytes 884744 | tf_op jit(solution)/shard_map/ppermute | solution.py:44
  108.7 10.2 %collective-permute-start.20 = (bf16[128,2048]{1,0:T(8,128)(2,1)}, bf16[128,2048]{1,0:T(8,128)(2,1)}, u32[]{:S(2)}, u32[]{:S(2)}) collective-permute-start(bf16[128,2048]{1,0:T(8,128)(2,1)} %get-tuple-element.72), channel_id=1, source_target_pairs={{0,64},{1,17},{2,66},{3,19},{4,68},{5,21},{6,70},{7,23},{8,72},{9,... | collective-permute-start | bytes 1572872 | tf_op jit(solution)/shard_map/ppermute | solution.py:364
  109.2 13.2 %collective-permute-start.21 = (bf16[128,2048]{1,0:T(8,128)(2,1)}, bf16[128,2048]{1,0:T(8,128)(2,1)}, u32[]{:S(2)}, u32[]{:S(2)}) collective-permute-start(bf16[128,2048]{1,0:T(8,128)(2,1)} %get-tuple-element.74), channel_id=1, source_target_pairs={{0,96},{1,25},{2,98},{3,27},{4,100},{5,29},{6,102},{7,31},{8,104},... | collective-permute-start | bytes 1572872 | tf_op jit(solution)/shard_map/ppermute | solution.py:364
  111.4 13.1 %collective-permute-start.22 = (bf16[128,2048]{1,0:T(8,128)(2,1)}, bf16[128,2048]{1,0:T(8,128)(2,1)}, u32[]{:S(2)}, u32[]{:S(2)}) collective-permute-start(bf16[128,2048]{1,0:T(8,128)(2,1)} %get-tuple-element.73), channel_id=1, source_target_pairs={{0,32},{1,9},{2,34},{3,11},{4,36},{5,13},{6,38},{7,15},{8,40},{9,1... | collective-permute-start | bytes 1572872 | tf_op jit(solution)/shard_map/ppermute | solution.py:364
  126.9 13.2 %all-to-all-start.2 = ((bf16[16,8,2048]{2,1,0:T(8,128)(2,1)}), bf16[16,8,2048]{2,1,0:T(8,128)(2,1)S(1)}, u32[]{:S(2)}, u32[]{:S(2)}) async-start(bf16[16,8,2048]{2,1,0:T(8,128)(2,1)} %fusion), calls=%async_computation.2 | async-start | bytes 1048576 | tf_op jit(solution)/shard_map/all_to_all | solution.py:365
  140.2 2.7 %collective-permute-start.23 = (bf16[4,2048]{1,0:T(4,128)(2,1)S(1)}, bf16[4,2048]{1,0:T(4,128)(2,1)S(1)}, u32[]{:S(2)}, u32[]{:S(2)}) collective-permute-start(bf16[4,2048]{1,0:T(4,128)(2,1)S(1)} %get-tuple-element.80), channel_id=1, source_target_pairs={{0,1},{1,0},{2,3},{3,2},{4,5},{5,4},{6,7},{7,6},{8,9},{9,8},{10,11... | collective-permute-start | bytes 49160 | tf_op jit(solution)/shard_map/ppermute | solution.py:44
  (20 other events, 166.0 us)
where the time goes:
time: 144 us
  starting transfers between devices  34.8 us (24%)
  Pallas kernels  31.1 us (22%)
  waiting for transfers between devices  28.4 us (20%)
  blocking collectives  17.6 us (12%)
  local copies, waits for them, and re-layouts  13 us (9%)
  matrix products  12 us (8%)
  other arithmetic  5.72 us (4%)
    pallas_call x2, Pallas kernels, logits_call(): pl.pallas_call(kernel, grid_spec=pltpu.PrefetchScalarGridSpec(num_scalar_...  19.2 us
    all_to_all x1, blocking collectives, body(): lax.all_to_all(message, AXES, 0, 0, axis_index_groups=CORES, tiled=True)  17.6 us
    ppermute x15, starting transfers between devices, swap(): return lax.ppermute(value, AXES, SWAP)  11.5 us
    ppermute x3, waiting for transfers between devices, body(): lax.ppermute(blocks[step], AXES, along(SIDE - step)).astype(f32)  11.1 us
    all_to_all x1, waiting for transfers between devices, body(): lax.all_to_all(wide, AXES, 0, 0, axis_index_groups=PLANES, tiled=True)  10.1 us
    pallas_call x1, Pallas kernels, turn_call(): pl.pallas_call(turn_kernel, grid_spec=pltpu.PrefetchScalarGridSpec(num_sc...  9.21 us
    dot_general x1, matrix products, body(): lax.dot_general(rows, grad, (((0,), (0,)), ((), ())), preferred_element_t...  8.38 us
    all_to_all x1, starting transfers between devices, body(): lax.all_to_all(wide, AXES, 0, 0, axis_index_groups=PLANES, tiled=True)  7.85 us
  transfers between devices with their start and end apart: 26, of which 15 were waited for; matrix products, arithmetic and copies ran while one was open for 11% of the time, Pallas kernels for 12%

commit v1 on v0

--- a/solution.py
+++ b/solution.py
@@ -9,7 +9,7 @@
 LOSS_SCALE = 64.0
 SIDE = 4
 CHIPS = SIDE**3
-LARGE, SMALL = 58 * 1024 * 1024, 16 * 1024 * 1024
+LARGE, SMALL = 58 * 1024 * 1024, 44 * 1024 * 1024
 STUDENT, TEACHER = 47 * 1024 * 1024, 53 * 1024 * 1024
 TILE = 256
 TILES = 3

time: 144 us -> 144 us (level)
  no operation moved by 1% of the time
where the time goes in v1:
time: 144 us; the launch traced here: 143 us
  starting transfers between devices  34.8 us (24%)
  Pallas kernels  31.1 us (22%)
  waiting for transfers between devices  28.4 us (20%)
  blocking collectives  17.6 us (12%)
  local copies, waits for them, and re-layouts  12.7 us (9%)
  matrix products  12 us (8%)
  other arithmetic  5.72 us (4%)
    pallas_call x2, Pallas kernels, logits_call(): pl.pallas_call(kernel, grid_spec=pltpu.PrefetchScalarGridSpec(num_scalar_...  19.2 us
    all_to_all x1, blocking collectives, body(): lax.all_to_all(message, AXES, 0, 0, axis_index_groups=CORES, tiled=True)  17.6 us
    ppermute x15, starting transfers between devices, swap(): return lax.ppermute(value, AXES, SWAP)  11.5 us
    ppermute x3, waiting for transfers between devices, body(): lax.ppermute(blocks[step], AXES, along(SIDE - step)).astype(f32)  11.1 us
    all_to_all x1, waiting for transfers between devices, body(): lax.all_to_all(wide, AXES, 0, 0, axis_index_groups=PLANES, tiled=True)  10.1 us
    pallas_call x1, Pallas kernels, turn_call(): pl.pallas_call(turn_kernel, grid_spec=pltpu.PrefetchScalarGridSpec(num_sc...  9.21 us
    dot_general x1, matrix products, body(): lax.dot_general(rows, grad, (((0,), (0,)), ((), ())), preferred_element_t...  8.39 us
    all_to_all x1, starting transfers between devices, body(): lax.all_to_all(wide, AXES, 0, 0, axis_index_groups=PLANES, tiled=True)  7.85 us
  transfers between devices with their start and end apart: 26, of which 15 were waited for; matrix products, arithmetic and copies ran while one was open for 11% of the time, Pallas kernels for 12%

profile of v1, /device:TPU:1, one launch (start us, length us, event | category | flops | bytes accessed | tf_op | source)
XLA Modules:
  0.0 143.2 jit_solution(18446352093606253207)
XLA Ops:
  1.6 1.5 %collective-permute-start = (bf16[8,2048]{1,0:T(8,128)(2,1)S(1)}, bf16[8,2048]{1,0:T(8,128)(2,1)S(1)}, u32[]{:S(2)}, u32[]{:S(2)}) collective-permute-start(bf16[8,2048]{1,0:T(8,128)(2,1)S(1)} %get-tuple-element.78), channel_id=1, source_target_pairs={{0,1},{1,0},{2,3},{3,2},{4,5},{5,4},{6,7},{7,6},{8,9},{9,8},{10,11... | collective-permute-start | bytes 98312 | tf_op jit(solution)/shard_map/ppermute | solution.py:44
  5.1 7.9 %all-to-all-start = ((bf16[16,2,8,2048]{3,2,1,0:T(8,128)(2,1)}), bf16[16,2,8,2048]{3,2,1,0:T(8,128)(2,1)S(1)}, u32[]{:S(2)}, u32[]{:S(2)}) async-start(bf16[16,2,8,2048]{3,2,1,0:T(8,128)(2,1)} %broadcast_in_dim.16), calls=%async_computation | async-start | bytes 2097152 | tf_op jit(solution)/shard_map/all_to_all | solution.py:298
  13.8 3.8 %constant_dynamic-slice_fusion.3 = bf16[2048,768]{1,0:T(8,128)(2,1)} fusion(bf16[4096,768]{1,0:T(8,128)(2,1)} %refs_8_.2, s32[]{:T(128)S(6)} %select_n.114), kind=kLoop, calls=%fused_computation.30 | loop fusion | bytes 6291460 | tf_op jit(solution)/shard_map/dynamic_slice | solution.py:304
  17.5 10.1 %all-to-all-done = bf16[16,2,8,2048]{3,2,1,0:T(8,128)(2,1)S(1)} async-done(((bf16[16,2,8,2048]{3,2,1,0:T(8,128)(2,1)}), bf16[16,2,8,2048]{3,2,1,0:T(8,128)(2,1)S(1)}, u32[]{:S(2)}, u32[]{:S(2)}) %all-to-all-start) | async-done | bytes 1048608 | tf_op jit(solution)/shard_map/all_to_all | solution.py:298
  29.1 2.2 %collective-permute-start.4 = (bf16[128,2048]{1,0:T(8,128)(2,1)S(1)}, bf16[128,2048]{1,0:T(8,128)(2,1)S(1)}, u32[]{:S(2)}, u32[]{:S(2)}) collective-permute-start(bf16[128,2048]{1,0:T(8,128)(2,1)S(1)} %get-tuple-element.39.refs_0_), channel_id=1, source_target_pairs={{0,96},{1,25},{2,98},{3,27},{4,100},{5,29},{6,102},{7,31},{8,104},... | collective-permute-start | bytes 1572872 | tf_op jit(solution)/shard_map/ppermute | solution.py:309
  31.3 1.7 %collective-permute-start.6 = (bf16[128,2048]{1,0:T(8,128)(2,1)S(1)}, bf16[128,2048]{1,0:T(8,128)(2,1)S(1)}, u32[]{:S(2)}, u32[]{:S(2)}) collective-permute-start(bf16[128,2048]{1,0:T(8,128)(2,1)S(1)} %get-tuple-element.39.refs_0_), channel_id=1, source_target_pairs={{0,64},{1,17},{2,66},{3,19},{4,68},{5,21},{6,70},{7,23},{8,72},{9,... | collective-permute-start | bytes 1572872 | tf_op jit(solution)/shard_map/ppermute | solution.py:312
  34.6 2.1 %collective-permute-start.1 = (bf16[128,2048]{1,0:T(8,128)(2,1)S(1)}, bf16[128,2048]{1,0:T(8,128)(2,1)S(1)}, u32[]{:S(2)}, u32[]{:S(2)}) collective-permute-start(bf16[128,2048]{1,0:T(8,128)(2,1)S(1)} %get-tuple-element.44.refs_0_), channel_id=1, source_target_pairs={{0,96},{1,25},{2,98},{3,27},{4,100},{5,29},{6,102},{7,31},{8,104},... | collective-permute-start | bytes 1572872 | tf_op jit(solution)/shard_map/ppermute | solution.py:309
  36.8 9.2 %shard_map.102 = bf16[1536,2048]{1,0:T(8,128)(2,1)} custom-call(s32[12]{0:T(128)} %concatenate.77.meta, bf16[4096,768]{1,0:T(8,128)(2,1)} %refs_8_.2, bf16[2048,768]{1,0:T(8,128)(2,1)} %collective-permute-done.7.far), custom_call_target="tpu_custom_call" | custom-call | bytes 12582912 | tf_op jit(solution)/shard_map/pallas_call | solution.py:190
  49.6 2.3 %collective-permute-start.3 = (bf16[128,2048]{1,0:T(8,128)(2,1)S(1)}, bf16[128,2048]{1,0:T(8,128)(2,1)S(1)}, u32[]{:S(2)}, u32[]{:S(2)}) collective-permute-start(bf16[128,2048]{1,0:T(8,128)(2,1)S(1)} %collective-permute-done.1.refs_1_), channel_id=1, source_target_pairs={{0,96},{1,25},{2,98},{3,27},{4,100},{5,29},{6,102},{7,31},{8,104},... | collective-permute-start | bytes 1572872 | tf_op jit(solution)/shard_map/ppermute | solution.py:311
  51.9 8.5 %shard_map.103 = (f32[512,768]{1,0:T(8,128)S(1)}, f32[512,768]{1,0:T(8,128)}, f32[8,512]{1,0:T(8,128)S(1)}, bf16[512,4096]{1,0:T(8,128)(2,1)}) custom-call(s32[12]{0:T(128)S(1)} %copy-done.3, bf16[128,2048]{1,0:T(8,128)(2,1)S(1)} %get-tuple-element.39.refs_0_, bf16[128,2048]{1,0:T(8,128)(2,1)S(1)} %collective-permute-done.4.refs_1_, ...), custom_call_target="tpu_custom_call" | custom-call | tf_op jit(solution)/shard_map/pallas_call | solution.py:158
  61.6 1.4 %collective-permute-start.13 = (bf16[128,2048]{1,0:T(8,128)(2,1)S(1)}, bf16[128,2048]{1,0:T(8,128)(2,1)S(1)}, u32[]{:S(2)}, u32[]{:S(2)}) collective-permute-start(bf16[128,2048]{1,0:T(8,128)(2,1)S(1)} %collective-permute-done.1.refs_1_), channel_id=1, source_target_pairs={{0,1},{1,0},{2,3},{3,2},{4,5},{5,4},{6,7},{7,6},{8,9},{9,8},{10,11... | collective-permute-start | bytes 1572872 | tf_op jit(solution)/shard_map/ppermute | solution.py:44
  66.9 10.7 %shard_map.104 = (f32[512,768]{1,0:T(8,128)}, f32[64,1,1152]{2,1,0:T(1,128)S(1)}) custom-call(s32[12]{0:T(128)S(1)} %copy-done.3, bf16[128,2048]{1,0:T(8,128)(2,1)} %copy-done.8, bf16[128,2048]{1,0:T(8,128)(2,1)} %copy-done.10, bf16[128,2048]{1,0:T(8,128)(2,1)} %copy-done.11, bf16[128,2048]{1,0:T(8,128)(2,1)} %copy-done.12, bf16[128,2048]{1,0:T(8,128)(2,1)} %copy-done.9, ...), custom_call_target="tpu_custom_call" | custom-call | tf_op jit(solution)/shard_map/pallas_call | solution.py:158
  78.2 17.6 %all_to_all.19.gathered = f32[64,1,1152]{2,1,0:T(1,128)S(1)} all-to-all(f32[64,1,1152]{2,1,0:T(1,128)S(1)} %get-tuple-element.53), channel_id=1, replica_groups={{0,2,4,6,8,10,12,14,16,18,20,22,24,26,28,30,32,34,36,38,40,42,44,46,48,..., dimensions={0} | all-to-all | bytes 589824 | tf_op jit(solution)/shard_map/all_to_all | solution.py:342
  95.8 1.6 %collective-permute-start.16 = (f32[64,1,1152]{2,1,0:T(1,128)S(1)}, f32[64,1,1152]{2,1,0:T(1,128)}, u32[]{:S(2)}, u32[]{:S(2)}) collective-permute-start(f32[64,1,1152]{2,1,0:T(1,128)S(1)} %all_to_all.19.gathered), channel_id=1, source_target_pairs={{0,1},{1,0},{2,3},{3,2},{4,5},{5,4},{6,7},{7,6},{8,9},{9,8},{10,11... | collective-permute-start | bytes 884744 | tf_op jit(solution)/shard_map/ppermute | solution.py:44
  100.2 2.8 %shard_map.105 = (bf16[512,768]{1,0:T(8,128)(2,1)S(1)}, bf16[512,1536]{1,0:T(8,128)(2,1)S(1)}, f32[8,512]{1,0:T(8,128)S(1)}) custom-call(s32[12]{0:T(128)S(1)} %copy-done.3, f32[512,768]{1,0:T(8,128)S(1)} %copy-done, f32[512,768]{1,0:T(8,128)S(1)} %copy-done.1, f32[512,768]{1,0:T(8,128)S(1)} %collective-permute-done.17.scaled_o, ...), custom_call_target="tpu_custom_call" | custom-call | flops 3932160 | bytes 7864320 | tf_op jit(solution)/shard_map/pallas_call | solution.py:347
  103.5 3.6 %convolution_convert_fusion.1 = bf16[512,2048]{1,0:T(8,128)(2,1)S(1)} fusion(bf16[512,1536]{1,0:T(8,128)(2,1)S(1)} %get-tuple-element.62, bf16[1536,2048]{1,0:T(8,128)(2,1)S(1)} %copy-done.7), kind=kOutput, calls=%fused_computation.2 | convolution fusion | flops 3222274048 | bytes 9961472 | tf_op jit(solution)/shard_map/dot_general | solution.py:360
  108.9 2.1 %collective-permute-start.21 = (bf16[128,2048]{1,0:T(8,128)(2,1)}, bf16[128,2048]{1,0:T(8,128)(2,1)}, u32[]{:S(2)}, u32[]{:S(2)}) collective-permute-start(bf16[128,2048]{1,0:T(8,128)(2,1)} %get-tuple-element.74), channel_id=1, source_target_pairs={{0,96},{1,25},{2,98},{3,27},{4,100},{5,29},{6,102},{7,31},{8,104},... | collective-permute-start | bytes 1572872 | tf_op jit(solution)/shard_map/ppermute | solution.py:364
  113.0 5.5 %collective-permute-done.20 = bf16[128,2048]{1,0:T(8,128)(2,1)} collective-permute-done((bf16[128,2048]{1,0:T(8,128)(2,1)}, bf16[128,2048]{1,0:T(8,128)(2,1)}, u32[]{:S(2)}, u32[]{:S(2)}) %collective-permute-start.20) | collective-permute-done | bytes 524320 | tf_op jit(solution)/shard_map/ppermute | solution.py:364
  118.5 3.6 %collective-permute-done.21 = bf16[128,2048]{1,0:T(8,128)(2,1)} collective-permute-done((bf16[128,2048]{1,0:T(8,128)(2,1)}, bf16[128,2048]{1,0:T(8,128)(2,1)}, u32[]{:S(2)}, u32[]{:S(2)}) %collective-permute-start.21) | collective-permute-done | bytes 524320 | tf_op jit(solution)/shard_map/ppermute | solution.py:364
  122.1 2.0 %collective-permute-done.22 = bf16[128,2048]{1,0:T(8,128)(2,1)} collective-permute-done((bf16[128,2048]{1,0:T(8,128)(2,1)}, bf16[128,2048]{1,0:T(8,128)(2,1)}, u32[]{:S(2)}, u32[]{:S(2)}) %collective-permute-start.22) | collective-permute-done | bytes 524320 | tf_op jit(solution)/shard_map/ppermute | solution.py:364
  124.1 2.5 %fusion = bf16[16,8,2048]{2,1,0:T(8,128)(2,1)} fusion(bf16[128,2048]{1,0:T(8,128)(2,1)} %collective-permute-done.22, bf16[128,2048]{1,0:T(8,128)(2,1)} %collective-permute-done.21, bf16[128,2048]{1,0:T(8,128)(2,1)} %collective-permute-done.20, bf16[512,2048]{1,0:T(8,128)(2,1)S(1)} %convolution_convert_fusion.1), kind=kLoop, calls=%fused_computation.4 | loop fusion | flops 2097152 | bytes 2621440 | tf_op jit(solution)/shard_map/all_to_all | solution.py:365
  126.6 3.6 %all-to-all-start.2 = ((bf16[16,8,2048]{2,1,0:T(8,128)(2,1)}), bf16[16,8,2048]{2,1,0:T(8,128)(2,1)S(1)}, u32[]{:S(2)}, u32[]{:S(2)}) async-start(bf16[16,8,2048]{2,1,0:T(8,128)(2,1)} %fusion), calls=%async_computation.2 | async-start | bytes 1048576 | tf_op jit(solution)/shard_map/all_to_all | solution.py:365
  130.2 8.4 %convolution_convert_fusion = bf16[4096,768]{1,0:T(8,128)(2,1)} fusion(bf16[512,4096]{1,0:T(8,128)(2,1)} %get-tuple-element.64, bf16[512,768]{1,0:T(8,128)(2,1)S(1)} %copy-done.5), kind=kOutput, calls=%fused_computation.1 | convolution fusion | flops 3224371200 | bytes 11272192 | tf_op jit(solution)/shard_map/dot_general | solution.py:366
  139.9 1.9 %collective-permute-start.23 = (bf16[4,2048]{1,0:T(4,128)(2,1)S(1)}, bf16[4,2048]{1,0:T(4,128)(2,1)S(1)}, u32[]{:S(2)}, u32[]{:S(2)}) collective-permute-start(bf16[4,2048]{1,0:T(4,128)(2,1)S(1)} %get-tuple-element.80), channel_id=1, source_target_pairs={{0,1},{1,0},{2,3},{3,2},{4,5},{5,4},{6,7},{7,6},{8,9},{9,8},{10,11... | collective-permute-start | bytes 49160 | tf_op jit(solution)/shard_map/ppermute | solution.py:44
  (101 shorter events, 25.8 us)
Async XLA Ops:
  1.6 2.4 %collective-permute-start = (bf16[8,2048]{1,0:T(8,128)(2,1)S(1)}, bf16[8,2048]{1,0:T(8,128)(2,1)S(1)}, u32[]{:S(2)}, u32[]{:S(2)}) collective-permute-start(bf16[8,2048]{1,0:T(8,128)(2,1)S(1)} %get-tuple-element.78), channel_id=1, source_target_pairs={{0,1},{1,0},{2,3},{3,2},{4,5},{5,4},{6,7},{7,6},{8,9},{9,8},{10,11... | collective-permute-start | bytes 98312 | tf_op jit(solution)/shard_map/ppermute | solution.py:44
  5.1 22.5 %all-to-all-start = ((bf16[16,2,8,2048]{3,2,1,0:T(8,128)(2,1)}), bf16[16,2,8,2048]{3,2,1,0:T(8,128)(2,1)S(1)}, u32[]{:S(2)}, u32[]{:S(2)}) async-start(bf16[16,2,8,2048]{3,2,1,0:T(8,128)(2,1)} %broadcast_in_dim.16), calls=%async_computation | async-start | bytes 2097152 | tf_op jit(solution)/shard_map/all_to_all | solution.py:298
  27.6 7.0 %collective-permute-start.7 = (bf16[2048,768]{1,0:T(8,128)(2,1)}, bf16[2048,768]{1,0:T(8,128)(2,1)}, u32[]{:S(2)}, u32[]{:S(2)}) collective-permute-start(bf16[2048,768]{1,0:T(8,128)(2,1)} %constant_dynamic-slice_fusion.3), channel_id=1, source_target_pairs={{0,1},{1,0},{2,3},{3,2},{4,5},{5,4},{6,7},{7,6},{8,9},{9,8},{10,11... | collective-permute-start | bytes 9437192 | tf_op jit(solution)/shard_map/ppermute | solution.py:44
  29.1 16.9 %collective-permute-start.4 = (bf16[128,2048]{1,0:T(8,128)(2,1)S(1)}, bf16[128,2048]{1,0:T(8,128)(2,1)S(1)}, u32[]{:S(2)}, u32[]{:S(2)}) collective-permute-start(bf16[128,2048]{1,0:T(8,128)(2,1)S(1)} %get-tuple-element.39.refs_0_), channel_id=1, source_target_pairs={{0,96},{1,25},{2,98},{3,27},{4,100},{5,29},{6,102},{7,31},{8,104},... | collective-permute-start | bytes 1572872 | tf_op jit(solution)/shard_map/ppermute | solution.py:309
  31.3 15.2 %collective-permute-start.5 = (bf16[128,2048]{1,0:T(8,128)(2,1)S(1)}, bf16[128,2048]{1,0:T(8,128)(2,1)S(1)}, u32[]{:S(2)}, u32[]{:S(2)}) collective-permute-start(bf16[128,2048]{1,0:T(8,128)(2,1)S(1)} %get-tuple-element.39.refs_0_), channel_id=1, source_target_pairs={{0,32},{1,9},{2,34},{3,11},{4,36},{5,13},{6,38},{7,15},{8,40},{9,1... | collective-permute-start | bytes 1572872 | tf_op jit(solution)/shard_map/ppermute | solution.py:309
  31.3 15.2 %collective-permute-start.6 = (bf16[128,2048]{1,0:T(8,128)(2,1)S(1)}, bf16[128,2048]{1,0:T(8,128)(2,1)S(1)}, u32[]{:S(2)}, u32[]{:S(2)}) collective-permute-start(bf16[128,2048]{1,0:T(8,128)(2,1)S(1)} %get-tuple-element.39.refs_0_), channel_id=1, source_target_pairs={{0,64},{1,17},{2,66},{3,19},{4,68},{5,21},{6,70},{7,23},{8,72},{9,... | collective-permute-start | bytes 1572872 | tf_op jit(solution)/shard_map/ppermute | solution.py:312
  33.0 13.4 %collective-permute-start.8 = (bf16[128,2048]{1,0:T(8,128)(2,1)S(1)}, bf16[128,2048]{1,0:T(8,128)(2,1)S(1)}, u32[]{:S(2)}, u32[]{:S(2)}) collective-permute-start(bf16[128,2048]{1,0:T(8,128)(2,1)S(1)} %get-tuple-element.44.refs_0_), channel_id=1, source_target_pairs={{0,1},{1,0},{2,3},{3,2},{4,5},{5,4},{6,7},{7,6},{8,9},{9,8},{10,11... | collective-permute-start | bytes 1572872 | tf_op jit(solution)/shard_map/ppermute | solution.py:44
  34.6 14.1 %collective-permute-start.1 = (bf16[128,2048]{1,0:T(8,128)(2,1)S(1)}, bf16[128,2048]{1,0:T(8,128)(2,1)S(1)}, u32[]{:S(2)}, u32[]{:S(2)}) collective-permute-start(bf16[128,2048]{1,0:T(8,128)(2,1)S(1)} %get-tuple-element.44.refs_0_), channel_id=1, source_target_pairs={{0,96},{1,25},{2,98},{3,27},{4,100},{5,29},{6,102},{7,31},{8,104},... | collective-permute-start | bytes 1572872 | tf_op jit(solution)/shard_map/ppermute | solution.py:309
  46.4 3.1 %collective-permute-start.10 = (bf16[128,2048]{1,0:T(8,128)(2,1)S(1)}, bf16[128,2048]{1,0:T(8,128)(2,1)S(1)}, u32[]{:S(2)}, u32[]{:S(2)}) collective-permute-start(bf16[128,2048]{1,0:T(8,128)(2,1)S(1)} %collective-permute-done.4.refs_1_), channel_id=1, source_target_pairs={{0,1},{1,0},{2,3},{3,2},{4,5},{5,4},{6,7},{7,6},{8,9},{9,8},{10,11... | collective-permute-start | bytes 1572872 | tf_op jit(solution)/shard_map/ppermute | solution.py:44
  47.6 4.3 %collective-permute-start.11 = (bf16[128,2048]{1,0:T(8,128)(2,1)S(1)}, bf16[128,2048]{1,0:T(8,128)(2,1)S(1)}, u32[]{:S(2)}, u32[]{:S(2)}) collective-permute-start(bf16[128,2048]{1,0:T(8,128)(2,1)S(1)} %collective-permute-done.5.refs_2_), channel_id=1, source_target_pairs={{0,1},{1,0},{2,3},{3,2},{4,5},{5,4},{6,7},{7,6},{8,9},{9,8},{10,11... | collective-permute-start | bytes 1572872 | tf_op jit(solution)/shard_map/ppermute | solution.py:44
  47.7 4.2 %collective-permute-start.12 = (bf16[128,2048]{1,0:T(8,128)(2,1)S(1)}, bf16[128,2048]{1,0:T(8,128)(2,1)S(1)}, u32[]{:S(2)}, u32[]{:S(2)}) collective-permute-start(bf16[128,2048]{1,0:T(8,128)(2,1)S(1)} %collective-permute-done.6.refs_3_), channel_id=1, source_target_pairs={{0,1},{1,0},{2,3},{3,2},{4,5},{5,4},{6,7},{7,6},{8,9},{9,8},{10,11... | collective-permute-start | bytes 1572872 | tf_op jit(solution)/shard_map/ppermute | solution.py:44
  48.1 3.8 %collective-permute-start.9 = (bf16[128,2048]{1,0:T(8,128)(2,1)S(1)}, bf16[128,2048]{1,0:T(8,128)(2,1)S(1)}, u32[]{:S(2)}, u32[]{:S(2)}) collective-permute-start(bf16[128,2048]{1,0:T(8,128)(2,1)S(1)} %get-tuple-element.39.refs_0_), channel_id=1, source_target_pairs={{0,1},{1,0},{2,3},{3,2},{4,5},{5,4},{6,7},{7,6},{8,9},{9,8},{10,11... | collective-permute-start | bytes 1572872 | tf_op jit(solution)/shard_map/ppermute | solution.py:44
  48.8 12.8 %collective-permute-start.2 = (bf16[128,2048]{1,0:T(8,128)(2,1)S(1)}, bf16[128,2048]{1,0:T(8,128)(2,1)S(1)}, u32[]{:S(2)}, u32[]{:S(2)}) collective-permute-start(bf16[128,2048]{1,0:T(8,128)(2,1)S(1)} %get-tuple-element.44.refs_0_), channel_id=1, source_target_pairs={{0,32},{1,9},{2,34},{3,11},{4,36},{5,13},{6,38},{7,15},{8,40},{9,1... | collective-permute-start | bytes 1572872 | tf_op jit(solution)/shard_map/ppermute | solution.py:309
  49.6 12.0 %collective-permute-start.3 = (bf16[128,2048]{1,0:T(8,128)(2,1)S(1)}, bf16[128,2048]{1,0:T(8,128)(2,1)S(1)}, u32[]{:S(2)}, u32[]{:S(2)}) collective-permute-start(bf16[128,2048]{1,0:T(8,128)(2,1)S(1)} %collective-permute-done.1.refs_1_), channel_id=1, source_target_pairs={{0,96},{1,25},{2,98},{3,27},{4,100},{5,29},{6,102},{7,31},{8,104},... | collective-permute-start | bytes 1572872 | tf_op jit(solution)/shard_map/ppermute | solution.py:311
  61.6 3.0 %collective-permute-start.13 = (bf16[128,2048]{1,0:T(8,128)(2,1)S(1)}, bf16[128,2048]{1,0:T(8,128)(2,1)S(1)}, u32[]{:S(2)}, u32[]{:S(2)}) collective-permute-start(bf16[128,2048]{1,0:T(8,128)(2,1)S(1)} %collective-permute-done.1.refs_1_), channel_id=1, source_target_pairs={{0,1},{1,0},{2,3},{3,2},{4,5},{5,4},{6,7},{7,6},{8,9},{9,8},{10,11... | collective-permute-start | bytes 1572872 | tf_op jit(solution)/shard_map/ppermute | solution.py:44
  63.2 2.9 %collective-permute-start.15 = (bf16[128,2048]{1,0:T(8,128)(2,1)S(1)}, bf16[128,2048]{1,0:T(8,128)(2,1)S(1)}, u32[]{:S(2)}, u32[]{:S(2)}) collective-permute-start(bf16[128,2048]{1,0:T(8,128)(2,1)S(1)} %collective-permute-done.3.refs_3_), channel_id=1, source_target_pairs={{0,1},{1,0},{2,3},{3,2},{4,5},{5,4},{6,7},{7,6},{8,9},{9,8},{10,11... | collective-permute-start | bytes 1572872 | tf_op jit(solution)/shard_map/ppermute | solution.py:44
  77.6 21.1 %collective-permute-start.17 = (f32[512,768]{1,0:T(8,128)S(1)}, f32[512,768]{1,0:T(8,128)S(1)}, u32[]{:S(2)}, u32[]{:S(2)}) collective-permute-start(f32[512,768]{1,0:T(8,128)S(1)} %copy-done), channel_id=1, source_target_pairs={{0,1},{1,0},{2,3},{3,2},{4,5},{5,4},{6,7},{7,6},{8,9},{9,8},{10,11... | collective-permute-start | bytes 4718600 | tf_op jit(solution)/shard_map/ppermute | solution.py:44
  78.1 20.7 %collective-permute-start.18 = (f32[512,768]{1,0:T(8,128)}, f32[512,768]{1,0:T(8,128)}, u32[]{:S(2)}, u32[]{:S(2)}) collective-permute-start(f32[512,768]{1,0:T(8,128)} %get-tuple-element.56.spread), channel_id=1, source_target_pairs={{0,1},{1,0},{2,3},{3,2},{4,5},{5,4},{6,7},{7,6},{8,9},{9,8},{10,11... | collective-permute-start | bytes 4718600 | tf_op jit(solution)/shard_map/ppermute | solution.py:44
  95.8 3.0 %collective-permute-start.16 = (f32[64,1,1152]{2,1,0:T(1,128)S(1)}, f32[64,1,1152]{2,1,0:T(1,128)}, u32[]{:S(2)}, u32[]{:S(2)}) collective-permute-start(f32[64,1,1152]{2,1,0:T(1,128)S(1)} %all_to_all.19.gathered), channel_id=1, source_target_pairs={{0,1},{1,0},{2,3},{3,2},{4,5},{5,4},{6,7},{7,6},{8,9},{9,8},{10,11... | collective-permute-start | bytes 884744 | tf_op jit(solution)/shard_map/ppermute | solution.py:44
  108.3 10.2 %collective-permute-start.20 = (bf16[128,2048]{1,0:T(8,128)(2,1)}, bf16[128,2048]{1,0:T(8,128)(2,1)}, u32[]{:S(2)}, u32[]{:S(2)}) collective-permute-start(bf16[128,2048]{1,0:T(8,128)(2,1)} %get-tuple-element.72), channel_id=1, source_target_pairs={{0,64},{1,17},{2,66},{3,19},{4,68},{5,21},{6,70},{7,23},{8,72},{9,... | collective-permute-start | bytes 1572872 | tf_op jit(solution)/shard_map/ppermute | solution.py:364
  108.9 13.2 %collective-permute-start.21 = (bf16[128,2048]{1,0:T(8,128)(2,1)}, bf16[128,2048]{1,0:T(8,128)(2,1)}, u32[]{:S(2)}, u32[]{:S(2)}) collective-permute-start(bf16[128,2048]{1,0:T(8,128)(2,1)} %get-tuple-element.74), channel_id=1, source_target_pairs={{0,96},{1,25},{2,98},{3,27},{4,100},{5,29},{6,102},{7,31},{8,104},... | collective-permute-start | bytes 1572872 | tf_op jit(solution)/shard_map/ppermute | solution.py:364
  111.0 13.1 %collective-permute-start.22 = (bf16[128,2048]{1,0:T(8,128)(2,1)}, bf16[128,2048]{1,0:T(8,128)(2,1)}, u32[]{:S(2)}, u32[]{:S(2)}) collective-permute-start(bf16[128,2048]{1,0:T(8,128)(2,1)} %get-tuple-element.73), channel_id=1, source_target_pairs={{0,32},{1,9},{2,34},{3,11},{4,36},{5,13},{6,38},{7,15},{8,40},{9,1... | collective-permute-start | bytes 1572872 | tf_op jit(solution)/shard_map/ppermute | solution.py:364
  126.6 13.2 %all-to-all-start.2 = ((bf16[16,8,2048]{2,1,0:T(8,128)(2,1)}), bf16[16,8,2048]{2,1,0:T(8,128)(2,1)S(1)}, u32[]{:S(2)}, u32[]{:S(2)}) async-start(bf16[16,8,2048]{2,1,0:T(8,128)(2,1)} %fusion), calls=%async_computation.2 | async-start | bytes 1048576 | tf_op jit(solution)/shard_map/all_to_all | solution.py:365
  139.9 2.7 %collective-permute-start.23 = (bf16[4,2048]{1,0:T(4,128)(2,1)S(1)}, bf16[4,2048]{1,0:T(4,128)(2,1)S(1)}, u32[]{:S(2)}, u32[]{:S(2)}) collective-permute-start(bf16[4,2048]{1,0:T(4,128)(2,1)S(1)} %get-tuple-element.80), channel_id=1, source_target_pairs={{0,1},{1,0},{2,3},{3,2},{4,5},{5,4},{6,7},{7,6},{8,9},{9,8},{10,11... | collective-permute-start | bytes 49160 | tf_op jit(solution)/shard_map/ppermute | solution.py:44
  (20 other events, 167.8 us)
